TPU v7x, 32 devices: a whole 2x2x4 slice. The times are simulated.
32 devices in a mesh: grp: 4 (over y, x), blk: 8 (over z, core).
Axes of the slice: x: 2, y: 2, z: 4, core: 2. Of those that a mesh axis runs over, the one named last changes fastest.
Arguments:
- queries: bfloat16 [4096, 4096], P(('grp', 'blk')), parts along dimension 0, may hold values from -256 to 256
- new_keys: bfloat16 [4096, 512], P(('grp', 'blk')), parts along dimension 0, may hold values from -6 to 6
- new_values: bfloat16 [4096, 512], P(('grp', 'blk')), parts along dimension 0, may hold values from -6 to 6
- prefix_keys: bfloat16 [4096, 512], P(('grp', 'blk')), parts along dimension 0, may hold values from -6 to 6
- prefix_values: bfloat16 [4096, 512], P(('grp', 'blk')), parts along dimension 0, may hold values from -6 to 6
- block_table: int32 [32, 8], P(('grp', 'blk')), parts along dimension 0, may hold values from 0 to 7, as said below
- prefix_blocks: int32 [32], P(('grp', 'blk')), parts along dimension 0, may hold values from 1 to 8, 40 in all
Outputs:
- attended: bfloat16 [4096, 4096], P(('grp', 'blk')), parts along dimension 0
There are 4 independent parts, one for each index of `grp`. A program takes and returns all parts, laid end to end along the dimension named above; each array names one. Nothing has to cross between parts.
Inputs may be any that keep to these rules, and one draw needn't show every extreme that they name: `block_table`: each row names 8 different prefix blocks; only the first prefix_blocks entries of a row are read. `prefix_blocks`: within each group (each index of grp) the lengths sum to 40.
All inputs are finite; a program needn't handle non-finite values.
Results may differ from a plain program's by a relative error of at most 0.008.
Values may be sent and summed in bfloat16 or wider, within the bound.
A program may use at most 64 MiB of HBM per device.

v0:
```python
import jax
import jax.numpy as jnp
from jax import lax
from jax.sharding import PartitionSpec as P

KVH = 4
DH = 128
BS = 128
G = 8


def head_major(block, heads):
    rows = block.shape[0]
    return block.reshape(rows, heads, DH).transpose(1, 0, 2)


def absorb(carry, key_block, value_block, usable, query_heads):
    top, total, summed = carry
    scores = jnp.einsum(
        "krd,kld->krl", query_heads, key_block, preferred_element_type=jnp.float32
    ) * DH ** (-0.5)
    scores = jnp.where(usable, scores, -jnp.inf)
    new_top = jnp.maximum(top, jnp.max(scores, axis=-1))
    factor = jnp.exp(top - new_top)
    weights = jnp.exp(scores - new_top[..., None])
    total = factor * total + jnp.sum(weights, axis=-1)
    summed = factor[..., None] * summed + jnp.einsum(
        "krl,kld->krd",
        weights.astype(jnp.bfloat16),
        value_block,
        preferred_element_type=jnp.float32,
    )
    return (new_top, total, summed)


def body(queries, new_keys, new_values, prefix_keys, prefix_values, block_table, prefix_blocks):
    tokens = queries.shape[0]
    query_heads = (
        queries.reshape(tokens, KVH, G, DH).transpose(1, 2, 0, 3).reshape(KVH, G * tokens, DH)
    )
    own_keys = head_major(new_keys, KVH)
    own_values = head_major(new_values, KVH)
    scores = jnp.einsum(
        "krd,kld->krl", query_heads, own_keys, preferred_element_type=jnp.float32
    ) * DH ** (-0.5)
    row_token = jnp.arange(G * tokens, dtype=jnp.int32) % tokens
    causal = jnp.arange(tokens, dtype=jnp.int32)[None, :] <= row_token[:, None]
    scores = jnp.where(causal[None], scores, -jnp.inf)
    top = jnp.max(scores, axis=-1)
    weights = jnp.exp(scores - top[..., None])
    total = jnp.sum(weights, axis=-1)
    summed = jnp.einsum(
        "krl,kld->krd", weights.astype(jnp.bfloat16), own_values, preferred_element_type=jnp.float32
    )
    carry = (top, total, summed)
    table_row = block_table[0]
    length = prefix_blocks[0]
    entries = table_row.shape[0]
    pool_count = lax.axis_size("blk")
    live_entry = jnp.arange(entries, dtype=jnp.int32) < length
    matches = (table_row[None, :] == jnp.arange(pool_count, dtype=jnp.int32)[:, None]) & live_entry[
        None, :
    ]
    used = jnp.any(matches, axis=1)
    state = carry
    piece_keys = lax.all_gather(prefix_keys, "blk", axis=0, tiled=True)
    piece_values = lax.all_gather(prefix_values, "blk", axis=0, tiled=True)
    count = piece_keys.shape[0] // BS
    key_blocks = piece_keys.reshape(count, BS, KVH, DH).transpose(0, 2, 1, 3)
    value_blocks = piece_values.reshape(count, BS, KVH, DH).transpose(0, 2, 1, 3)
    block_ids = jnp.arange(count, dtype=jnp.int32)

    def visit(inner, items):
        key_block, value_block, block_id = items
        return (absorb(inner, key_block, value_block, used[block_id], query_heads), None)

    state, _ = lax.scan(visit, state, (key_blocks, value_blocks, block_ids))
    carry = state
    top, total, summed = carry
    result = summed / total[..., None]
    result = result.reshape(KVH, G, tokens, DH).transpose(2, 0, 1, 3).reshape(tokens, KVH * G * DH)
    return result.astype(jnp.bfloat16)


def solution(mesh):
    in_specs = (
        P(("grp", "blk"), None),
        P(("grp", "blk"), None),
        P(("grp", "blk"), None),
        P(("grp", "blk"), None),
        P(("grp", "blk"), None),
        P(("grp", "blk"), None),
        P(("grp", "blk")),
    )
    out_specs = P(("grp", "blk"), None)
    return jax.shard_map(body, mesh=mesh, in_specs=in_specs, out_specs=out_specs, check_vma=False)
```

profile of v0, /device:TPU:0, one launch (start us, length us, event | category | flops | bytes accessed | tf_op | source)
XLA Modules:
  0.0 144.2 jit_solution(12270242743546062695)
XLA Ops:
  6.5 0.0 copy-start
  6.5 0.0 all-gather.5.cloned.1.call-start
  6.5 0.7 all-gather.5.cloned.1.call-update
  7.3 0.0 all-gather.3.cloned.1.call-start
  7.3 0.7 all-gather.3.cloned.1.call-update
  8.0 0.0 copy-start.2
  8.0 1.4 %copy.42 = bf16[16,8,32,128]{3,2,1,0:T(8,128)(2,1)S(1)} copy(bf16[16,8,32,128]{3,1,2,0:T(8,128)(2,1)} %bitcast.93) | data formatting | bytes 2097152
  9.5 0.4 copy.25
  10.6 0.1 fusion.33
  10.7 0.1 iota_compare_fusion
  10.8 0.0 copy-start.1
  10.8 0.5 fusion.17
  11.3 0.5 fusion.19
  11.8 0.7 fusion.20
  12.6 21.2 %all-gather.5.cloned.1.call-done = bf16[1024,512]{1,0:T(8,128)(2,1)} async-done(((bf16[128,512]{1,0:T(8,128)(2,1)}), bf16[1024,512]{1,0:T(8,128)(2,1)}) %all-gather.5.cloned.1.call-update) | async-done | bytes 1048592 | tf_op jit(solution)/shard_map/all_gather | solution.py:67
  33.8 2.1 %reshape.65 = bf16[8,128,4,128]{3,2,1,0:T(4,128)(2,1)} reshape(bf16[1024,512]{1,0:T(8,128)(2,1)} %all-gather.5.cloned.1.call-done) | data formatting | bytes 2097152 | tf_op jit(solution)/shard_map/reshape | solution.py:70
  35.9 2.5 %copy.58 = bf16[8,128,4,128]{3,1,2,0:T(8,128)(2,1)} copy(bf16[8,128,4,128]{3,2,1,0:T(4,128)(2,1)} %reshape.65) | data formatting | bytes 2097152 | tf_op jit(solution)/shard_map/transpose | solution.py:70
  38.4 18.7 %all-gather.3.cloned.1.call-done = bf16[1024,512]{1,0:T(8,128)(2,1)} async-done(((bf16[128,512]{1,0:T(8,128)(2,1)}), bf16[1024,512]{1,0:T(8,128)(2,1)}) %all-gather.3.cloned.1.call-update) | async-done | bytes 1048592 | tf_op jit(solution)/shard_map/all_gather | solution.py:66
  57.1 2.1 %reshape.64 = bf16[8,128,4,128]{3,2,1,0:T(4,128)(2,1)} reshape(bf16[1024,512]{1,0:T(8,128)(2,1)} %all-gather.3.cloned.1.call-done) | data formatting | bytes 2097152 | tf_op jit(solution)/shard_map/reshape | solution.py:69
  59.3 2.5 %copy.59 = bf16[8,128,4,128]{3,1,2,0:T(8,128)(2,1)} copy(bf16[8,128,4,128]{3,2,1,0:T(4,128)(2,1)} %reshape.64) | data formatting | bytes 2097152 | tf_op jit(solution)/shard_map/transpose | solution.py:69
  61.8 72.7 %while.14 = (s32[]{:T(128)}, f32[4,1024]{1,0:T(4,128)S(1)}, f32[4,1024]{1,0:T(4,128)S(1)}, f32[4,1024,128]{2,1,0:T(8,128)S(1)}, s32[8]{0:T(128)S(1)}, /*index=5*...) while((s32[]{:T(128)}, f32[4,1024]{1,0:T(4,128)S(1)}, ...), condition=%wide.region_6.7_spmd, body=%wide.region_3.6_spmd.sunk | while | flops 275259392 | bytes 12060842 | solution.py:77
  61.8 0.6 dynamic_slice.30
  64.3 0.6 dynamic_slice.31
  64.9 2.0 %bitcast_reduce_fusion.2 = (f32[4,1024]{1,0:T(4,128)S(1)}, f32[4,128,1024]{2,1,0:T(8,128)S(1)}) fusion(pred[]{:T(512)} %bitcast.84, bf16[4,1024,128]{2,1,0:T(8,128)(2,1)S(1)} %get-tuple-element.191, bf16[8,4,128,128]{3,2,1,0:T(8,128)(2,1)} %get-tuple-element.190, s32[]{:T(128)} %get-tuple-element.172), kind=kOutput, calls=%fused_computation.1.clone.1 | convolution fusion | flops 135786496 | bytes 3294208 | tf_op jit(solution)/shard_map/while/body/eval_jaxpr/krd,kld->krl/dot_general | solution.py:19
  66.9 1.1 fusion.47
  68.1 2.8 %multiply_add_fusion.5 = f32[4,1024,128]{2,1,0:T(8,128)S(1)} fusion(f32[4,1024,128]{2,1,0:T(8,128)S(1)} %get-tuple-element.175, f32[4,128,1024]{2,1,0:T(8,128)S(1)} %get-tuple-element.157, f32[4,1024]{1,0:T(4,128)S(1)} %get-tuple-element.159, f32[4,1024]{1,0:T(4,128)S(1)} %max.4, pred[]{:T(512)} %bitcast.84, ...), kind=kOutput, calls=%fused_computation.3.clone.1 | convolution fusion | flops 137363456 | bytes 6456320 | tf_op jit(solution)/shard_map/while/body/eval_jaxpr/krl,kld->krd/dot_general | solution.py:27
  70.9 0.6 dynamic_slice.30
  73.4 0.6 dynamic_slice.31
  74.0 2.0 %bitcast_reduce_fusion.2 = (f32[4,1024]{1,0:T(4,128)S(1)}, f32[4,128,1024]{2,1,0:T(8,128)S(1)}) fusion(pred[]{:T(512)} %bitcast.84, bf16[4,1024,128]{2,1,0:T(8,128)(2,1)S(1)} %get-tuple-element.191, bf16[8,4,128,128]{3,2,1,0:T(8,128)(2,1)} %get-tuple-element.190, s32[]{:T(128)} %get-tuple-element.172), kind=kOutput, calls=%fused_computation.1.clone.1 | convolution fusion | flops 135786496 | bytes 3294208 | tf_op jit(solution)/shard_map/while/body/eval_jaxpr/krd,kld->krl/dot_general | solution.py:19
  76.0 1.1 fusion.47
  77.2 2.8 %multiply_add_fusion.5 = f32[4,1024,128]{2,1,0:T(8,128)S(1)} fusion(f32[4,1024,128]{2,1,0:T(8,128)S(1)} %get-tuple-element.175, f32[4,128,1024]{2,1,0:T(8,128)S(1)} %get-tuple-element.157, f32[4,1024]{1,0:T(4,128)S(1)} %get-tuple-element.159, f32[4,1024]{1,0:T(4,128)S(1)} %max.4, pred[]{:T(512)} %bitcast.84, ...), kind=kOutput, calls=%fused_computation.3.clone.1 | convolution fusion | flops 137363456 | bytes 6456320 | tf_op jit(solution)/shard_map/while/body/eval_jaxpr/krl,kld->krd/dot_general | solution.py:27
  80.0 0.6 dynamic_slice.30
  82.5 0.6 dynamic_slice.31
  83.1 2.0 %bitcast_reduce_fusion.2 = (f32[4,1024]{1,0:T(4,128)S(1)}, f32[4,128,1024]{2,1,0:T(8,128)S(1)}) fusion(pred[]{:T(512)} %bitcast.84, bf16[4,1024,128]{2,1,0:T(8,128)(2,1)S(1)} %get-tuple-element.191, bf16[8,4,128,128]{3,2,1,0:T(8,128)(2,1)} %get-tuple-element.190, s32[]{:T(128)} %get-tuple-element.172), kind=kOutput, calls=%fused_computation.1.clone.1 | convolution fusion | flops 135786496 | bytes 3294208 | tf_op jit(solution)/shard_map/while/body/eval_jaxpr/krd,kld->krl/dot_general | solution.py:19
  85.1 1.1 fusion.47
  86.2 2.8 %multiply_add_fusion.5 = f32[4,1024,128]{2,1,0:T(8,128)S(1)} fusion(f32[4,1024,128]{2,1,0:T(8,128)S(1)} %get-tuple-element.175, f32[4,128,1024]{2,1,0:T(8,128)S(1)} %get-tuple-element.157, f32[4,1024]{1,0:T(4,128)S(1)} %get-tuple-element.159, f32[4,1024]{1,0:T(4,128)S(1)} %max.4, pred[]{:T(512)} %bitcast.84, ...), kind=kOutput, calls=%fused_computation.3.clone.1 | convolution fusion | flops 137363456 | bytes 6456320 | tf_op jit(solution)/shard_map/while/body/eval_jaxpr/krl,kld->krd/dot_general | solution.py:27
  89.1 0.6 dynamic_slice.30
  91.6 0.6 dynamic_slice.31
  92.2 2.0 %bitcast_reduce_fusion.2 = (f32[4,1024]{1,0:T(4,128)S(1)}, f32[4,128,1024]{2,1,0:T(8,128)S(1)}) fusion(pred[]{:T(512)} %bitcast.84, bf16[4,1024,128]{2,1,0:T(8,128)(2,1)S(1)} %get-tuple-element.191, bf16[8,4,128,128]{3,2,1,0:T(8,128)(2,1)} %get-tuple-element.190, s32[]{:T(128)} %get-tuple-element.172), kind=kOutput, calls=%fused_computation.1.clone.1 | convolution fusion | flops 135786496 | bytes 3294208 | tf_op jit(solution)/shard_map/while/body/eval_jaxpr/krd,kld->krl/dot_general | solution.py:19
  94.2 1.1 fusion.47
  95.3 2.8 %multiply_add_fusion.5 = f32[4,1024,128]{2,1,0:T(8,128)S(1)} fusion(f32[4,1024,128]{2,1,0:T(8,128)S(1)} %get-tuple-element.175, f32[4,128,1024]{2,1,0:T(8,128)S(1)} %get-tuple-element.157, f32[4,1024]{1,0:T(4,128)S(1)} %get-tuple-element.159, f32[4,1024]{1,0:T(4,128)S(1)} %max.4, pred[]{:T(512)} %bitcast.84, ...), kind=kOutput, calls=%fused_computation.3.clone.1 | convolution fusion | flops 137363456 | bytes 6456320 | tf_op jit(solution)/shard_map/while/body/eval_jaxpr/krl,kld->krd/dot_general | solution.py:27
  98.1 0.6 dynamic_slice.30
  100.7 0.6 dynamic_slice.31
  101.3 2.0 %bitcast_reduce_fusion.2 = (f32[4,1024]{1,0:T(4,128)S(1)}, f32[4,128,1024]{2,1,0:T(8,128)S(1)}) fusion(pred[]{:T(512)} %bitcast.84, bf16[4,1024,128]{2,1,0:T(8,128)(2,1)S(1)} %get-tuple-element.191, bf16[8,4,128,128]{3,2,1,0:T(8,128)(2,1)} %get-tuple-element.190, s32[]{:T(128)} %get-tuple-element.172), kind=kOutput, calls=%fused_computation.1.clone.1 | convolution fusion | flops 135786496 | bytes 3294208 | tf_op jit(solution)/shard_map/while/body/eval_jaxpr/krd,kld->krl/dot_general | solution.py:19
  103.3 1.1 fusion.47
  104.4 2.8 %multiply_add_fusion.5 = f32[4,1024,128]{2,1,0:T(8,128)S(1)} fusion(f32[4,1024,128]{2,1,0:T(8,128)S(1)} %get-tuple-element.175, f32[4,128,1024]{2,1,0:T(8,128)S(1)} %get-tuple-element.157, f32[4,1024]{1,0:T(4,128)S(1)} %get-tuple-element.159, f32[4,1024]{1,0:T(4,128)S(1)} %max.4, pred[]{:T(512)} %bitcast.84, ...), kind=kOutput, calls=%fused_computation.3.clone.1 | convolution fusion | flops 137363456 | bytes 6456320 | tf_op jit(solution)/shard_map/while/body/eval_jaxpr/krl,kld->krd/dot_general | solution.py:27
  107.2 0.6 dynamic_slice.30
  109.8 0.6 dynamic_slice.31
  110.3 2.0 %bitcast_reduce_fusion.2 = (f32[4,1024]{1,0:T(4,128)S(1)}, f32[4,128,1024]{2,1,0:T(8,128)S(1)}) fusion(pred[]{:T(512)} %bitcast.84, bf16[4,1024,128]{2,1,0:T(8,128)(2,1)S(1)} %get-tuple-element.191, bf16[8,4,128,128]{3,2,1,0:T(8,128)(2,1)} %get-tuple-element.190, s32[]{:T(128)} %get-tuple-element.172), kind=kOutput, calls=%fused_computation.1.clone.1 | convolution fusion | flops 135786496 | bytes 3294208 | tf_op jit(solution)/shard_map/while/body/eval_jaxpr/krd,kld->krl/dot_general | solution.py:19
  112.4 1.1 fusion.47
  113.5 2.8 %multiply_add_fusion.5 = f32[4,1024,128]{2,1,0:T(8,128)S(1)} fusion(f32[4,1024,128]{2,1,0:T(8,128)S(1)} %get-tuple-element.175, f32[4,128,1024]{2,1,0:T(8,128)S(1)} %get-tuple-element.157, f32[4,1024]{1,0:T(4,128)S(1)} %get-tuple-element.159, f32[4,1024]{1,0:T(4,128)S(1)} %max.4, pred[]{:T(512)} %bitcast.84, ...), kind=kOutput, calls=%fused_computation.3.clone.1 | convolution fusion | flops 137363456 | bytes 6456320 | tf_op jit(solution)/shard_map/while/body/eval_jaxpr/krl,kld->krd/dot_general | solution.py:27
  116.3 0.6 dynamic_slice.30
  118.8 0.6 dynamic_slice.31
  119.4 2.0 %bitcast_reduce_fusion.2 = (f32[4,1024]{1,0:T(4,128)S(1)}, f32[4,128,1024]{2,1,0:T(8,128)S(1)}) fusion(pred[]{:T(512)} %bitcast.84, bf16[4,1024,128]{2,1,0:T(8,128)(2,1)S(1)} %get-tuple-element.191, bf16[8,4,128,128]{3,2,1,0:T(8,128)(2,1)} %get-tuple-element.190, s32[]{:T(128)} %get-tuple-element.172), kind=kOutput, calls=%fused_computation.1.clone.1 | convolution fusion | flops 135786496 | bytes 3294208 | tf_op jit(solution)/shard_map/while/body/eval_jaxpr/krd,kld->krl/dot_general | solution.py:19
  121.5 1.1 fusion.47
  122.6 2.8 %multiply_add_fusion.5 = f32[4,1024,128]{2,1,0:T(8,128)S(1)} fusion(f32[4,1024,128]{2,1,0:T(8,128)S(1)} %get-tuple-element.175, f32[4,128,1024]{2,1,0:T(8,128)S(1)} %get-tuple-element.157, f32[4,1024]{1,0:T(4,128)S(1)} %get-tuple-element.159, f32[4,1024]{1,0:T(4,128)S(1)} %max.4, pred[]{:T(512)} %bitcast.84, ...), kind=kOutput, calls=%fused_computation.3.clone.1 | convolution fusion | flops 137363456 | bytes 6456320 | tf_op jit(solution)/shard_map/while/body/eval_jaxpr/krl,kld->krd/dot_general | solution.py:27
  125.4 0.6 dynamic_slice.30
  127.9 0.6 dynamic_slice.31
  128.5 2.0 %bitcast_reduce_fusion.2 = (f32[4,1024]{1,0:T(4,128)S(1)}, f32[4,128,1024]{2,1,0:T(8,128)S(1)}) fusion(pred[]{:T(512)} %bitcast.84, bf16[4,1024,128]{2,1,0:T(8,128)(2,1)S(1)} %get-tuple-element.191, bf16[8,4,128,128]{3,2,1,0:T(8,128)(2,1)} %get-tuple-element.190, s32[]{:T(128)} %get-tuple-element.172), kind=kOutput, calls=%fused_computation.1.clone.1 | convolution fusion | flops 135786496 | bytes 3294208 | tf_op jit(solution)/shard_map/while/body/eval_jaxpr/krd,kld->krl/dot_general | solution.py:19
  130.5 1.1 fusion.47
  131.7 2.8 %multiply_add_fusion.5 = f32[4,1024,128]{2,1,0:T(8,128)S(1)} fusion(f32[4,1024,128]{2,1,0:T(8,128)S(1)} %get-tuple-element.175, f32[4,128,1024]{2,1,0:T(8,128)S(1)} %get-tuple-element.157, f32[4,1024]{1,0:T(4,128)S(1)} %get-tuple-element.159, f32[4,1024]{1,0:T(4,128)S(1)} %max.4, pred[]{:T(512)} %bitcast.84, ...), kind=kOutput, calls=%fused_computation.3.clone.1 | convolution fusion | flops 137363456 | bytes 6456320 | tf_op jit(solution)/shard_map/while/body/eval_jaxpr/krl,kld->krd/dot_general | solution.py:27
  134.5 0.7 divide_convert_fusion
  135.2 0.7 copy.33
  135.9 1.4 copy.57
  (30 shorter events, 0.3 us)
Async XLA Ops:
  6.5 4.2 %copy-start = (bf16[128,512]{1,0:T(8,128)(2,1)S(1)}, bf16[128,512]{1,0:T(8,128)(2,1)}, u32[]{:S(2)}) copy-start(bf16[128,512]{1,0:T(8,128)(2,1)} %param.10) | copy-start | bytes 393220
  6.5 27.3 %all-gather.5.cloned.1.call-start = ((), (), s32[]{:S(2)}) async-start(), calls=%async_computation.1 | async-start | bytes 1179648 | tf_op jit(solution)/shard_map/all_gather | solution.py:67
  7.3 49.9 %all-gather.3.cloned.1.call-start = ((), (), s32[]{:S(2)}) async-start(), calls=%async_computation | async-start | bytes 1179648 | tf_op jit(solution)/shard_map/all_gather | solution.py:66
  8.0 2.6 %copy-start.2 = (s32[1,8]{1,0:T(1,128)S(1)}, s32[1,8]{1,0:T(1,128)}, u32[]{:S(2)}) copy-start(s32[1,8]{1,0:T(1,128)} %param.14) | copy-start | bytes 100
  10.8 1.0 copy-start.1
Sparse Core Ops, SparseCore 0:
  9.0 24.7 all-gather.4
  35.4 21.7 all-gather.2
where the time goes:
time: 145 us; the launch traced here: 144 us
  waiting for transfers between devices  41.4 us (29%)
  matrix products  39.5 us (27%)
  local copies, waits for them, and re-layouts  22.7 us (16%)
  loops' own time  16 us (11%)
  between operations  14.2 us (10%)
  other arithmetic  10.4 us (7%)
    dot_general x8, matrix products, absorb(): jnp.einsum('krl,kld->krd', weights.astype(jnp.bfloat16), value_block, pre...  22.2 us
    all_gather x1, waiting for transfers between devices, body(): piece_values = lax.all_gather(prefix_values, 'blk', axis=0, tiled=True)  21.2 us
    all_gather x1, waiting for transfers between devices, body(): piece_keys = lax.all_gather(prefix_keys, 'blk', axis=0, tiled=True)  18.7 us
    dot_general x8, matrix products, absorb(): jnp.einsum('krd,kld->krl', query_heads, key_block, preferred_element_type...  16 us
    another operation x1, loops' own time, body(): state, _ = lax.scan(visit, state, (key_blocks, value_blocks, block_ids))  16 us
    reduce_sum x8, other arithmetic, absorb(): total = factor * total + jnp.sum(weights, axis=-1)  8.78 us
    dynamic_slice x8, local copies, waits for them, and re-layouts, visit(): used[block_id]  4.71 us
    dynamic_slice x8, local copies, waits for them, and re-layouts, body(): state, _ = lax.scan(visit, state, (key_blocks, value_blocks, block_ids))  4.69 us
  transfers between devices with their start and end apart: 2, of which 2 were waited for; matrix products, arithmetic and copies ran while one was open for 6% of the time, Pallas kernels for 0%

commit v1 on v0

v1 whole, which is shorter than its diff:
```python
import functools

import jax
import jax.numpy as jnp
from jax import lax
from jax.experimental import pallas as pl
from jax.experimental.pallas import tpu as pltpu
from jax.sharding import PartitionSpec as P

DH = 128
BS = 128
MESH = pl.DeviceIdType.MESH
LOG2E = 1.4426950408889634
HIDDEN = 1e38
ROWS = 256


def kernel(
    chips, kvh, group, entries,
    table_ref, length_ref, q_hbm, nk_hbm, nv_hbm, pk_hbm, pv_hbm, out_hbm,
    qs, own, kv, acc, top, total, out, penalty,
    q_sem, own_sem, load_sem, out_sem, recv_line, recv_pair, send_line, send_right, send_pair,
):
    me = lax.axis_index("blk")
    chip = me // 2
    core = me - 2 * chip
    partner = 2 * chip + 1 - core
    rows = group * BS
    factor = LOG2E * DH ** -0.5
    has_left, has_right = chip > 0, chip < chips - 1

    barrier = pltpu.get_barrier_semaphore()

    def greet(device):
        pl.semaphore_signal(barrier, inc=1, device_id={"blk": device}, device_id_type=MESH)

    greet(partner)
    pl.when(has_left)(lambda: greet(me - 2))
    pl.when(has_right)(lambda: greet(me + 2))

    for h in range(kvh):
        cols = pl.ds(h * DH, DH)
        pltpu.make_async_copy(pk_hbm.at[:, cols], kv.at[chip, h, 0, core], load_sem.at[h]).start()
        pltpu.make_async_copy(pv_hbm.at[:, cols], kv.at[chip, h, 1, core], load_sem.at[h]).start()
    for h in range(kvh):
        cols = pl.ds(h * DH, DH)
        pltpu.make_async_copy(nk_hbm.at[:, cols], own.at[h, 0], own_sem.at[h]).start()
        pltpu.make_async_copy(nv_hbm.at[:, cols], own.at[h, 1], own_sem.at[h]).start()
        for g in range(group):
            pltpu.make_async_copy(
                q_hbm.at[:, pl.ds((h * group + g) * DH, DH)], qs.at[h, pl.ds(g * BS, BS)], q_sem.at[h]
            ).start()

    def line_copy(source, h, device, sem):
        piece = kv.at[source, h, :, core]
        return pltpu.make_async_remote_copy(
            src_ref=piece, dst_ref=piece, send_sem=sem, recv_sem=recv_line.at[source, h],
            device_id={"blk": device}, device_id_type=MESH,
        )

    def pair_copy(source, h):
        piece = kv.at[source, h, :, core]
        return pltpu.make_async_remote_copy(
            src_ref=piece, dst_ref=piece, send_sem=send_pair.at[source, h], recv_sem=recv_pair.at[source, h],
            device_id={"blk": partner}, device_id_type=MESH,
        )

    def to_left(source, h):
        return line_copy(source, h, me - 2, send_line.at[source, h])

    def to_right(source, h):
        return line_copy(source, h, me + 2, send_line.at[source, h])

    def own_right(h):
        return line_copy(chip, h, me + 2, send_right.at[h])

    pl.semaphore_wait(barrier, 1 + has_left.astype(jnp.int32) + has_right.astype(jnp.int32))
    for h in range(kvh):
        piece = kv.at[chip, h, :, core]
        pltpu.make_async_copy(piece, piece, load_sem.at[h]).wait()
        pl.when(has_left)(lambda: to_left(chip, h).start())
        pl.when(has_right)(lambda: own_right(h).start())
        pair_copy(chip, h).start()

    length = length_ref[0]
    for b in range(2 * chips):
        hits = [(table_ref[0, j] == b) & (j < length) for j in range(entries)]
        penalty[b] = jnp.where(functools.reduce(jnp.logical_or, hits), 0.0, HIDDEN)

    def scores_of(query, keys):
        return lax.dot_general(query, keys, (((1,), (1,)), ((), ())), preferred_element_type=jnp.float32)

    def own_tokens(h, _):
        pltpu.make_async_copy(qs.at[h], qs.at[h], q_sem.at[h]).wait()
        pltpu.make_async_copy(own.at[h], own.at[h], own_sem.at[h]).wait()
        keys, values = own[h, 0], own[h, 1]
        token = lax.broadcasted_iota(jnp.int32, (ROWS, BS), 0) % BS
        causal = lax.broadcasted_iota(jnp.int32, (ROWS, BS), 1) <= token
        for r in range(0, rows, ROWS):
            at = pl.ds(r, ROWS)
            scores = jnp.where(causal, scores_of(qs[h, at], keys), -HIDDEN)
            best = jnp.broadcast_to(jnp.max(scores, axis=-1, keepdims=True), (ROWS, DH))
            weights = jnp.exp2((scores - best) * factor)
            top[h, at] = best
            total[h, at] = weights
            acc[h, at] = jnp.dot(weights.astype(jnp.bfloat16), values, preferred_element_type=jnp.float32)
        return 0

    def absorb(source, h):
        keys = kv[source, h, 0].reshape(2 * BS, DH)
        values = kv[source, h, 1].reshape(2 * BS, DH)
        low, high = penalty[2 * source], penalty[2 * source + 1]
        for r in range(0, rows, ROWS):
            at = pl.ds(r, ROWS)
            scores = scores_of(qs[h, at], keys)
            first, second = scores[:, :BS] - low, scores[:, BS:] - high
            old = top[h, at]
            best = jnp.max(jnp.maximum(first, second), axis=-1, keepdims=True)
            best = jnp.maximum(old, jnp.broadcast_to(best, (ROWS, DH)))
            shrink = jnp.exp2((old - best) * factor)
            first = jnp.exp2((first - best) * factor)
            second = jnp.exp2((second - best) * factor)
            top[h, at] = best
            total[h, at] = shrink * total[h, at] + (first + second)
            weights = jnp.concatenate([first.astype(jnp.bfloat16), second.astype(jnp.bfloat16)], axis=1)
            acc[h, at] = shrink * acc[h, at] + jnp.dot(weights, values, preferred_element_type=jnp.float32)

    def out_copy(h):
        cols = pl.ds(pl.multiple_of(h * rows, DH), rows)
        return pltpu.make_async_copy(out.at[h], out_hbm.at[:, cols], out_sem.at[h])

    def finish(h):
        for g in range(group):
            at = pl.ds(g * BS, BS)
            whole = jnp.sum(total[h, at], axis=-1, keepdims=True)
            out[h, :, g * DH:(g + 1) * DH] = (acc[h, at] / whole).astype(jnp.bfloat16)
        out_copy(h).start()

    def own_chip(h, _):
        pair_copy(chip, h).wait_recv()
        absorb(chip, h)
        return 0

    def forward(i):
        far, h = 1 + i // kvh, i % kvh
        before, after = chip - far, chip + far

        @pl.when(after < chips)
        def _():
            line_copy(after, h, partner, send_line.at[after, h]).wait_recv()
            pl.when(has_left)(lambda: to_left(after, h).start())
            pair_copy(after, h).start()

        @pl.when(before >= 0)
        def _():
            line_copy(before, h, partner, send_line.at[before, h]).wait_recv()
            pl.when(has_right)(lambda: to_right(before, h).start())
            pair_copy(before, h).start()

    def sent(far, h):
        before, after = chip - far, chip + far

        @pl.when(after < chips)
        def _():
            pl.when(has_left)(lambda: to_left(after, h).wait_send())
            pair_copy(after, h).wait_send()

        @pl.when(before >= 0)
        def _():
            pl.when(has_right)(lambda: to_right(before, h).wait_send())
            pair_copy(before, h).wait_send()

    def own_sent(h):
        pl.when(has_left)(lambda: to_left(chip, h).wait_send())
        pl.when(has_right)(lambda: own_right(h).wait_send())
        pair_copy(chip, h).wait_send()

    def step(i, _):
        far, h = 1 + i // kvh, i % kvh
        before, after = chip - far, chip + far
        pl.when(i + 1 < kvh * (chips - 1))(lambda: forward(i + 1))
        pl.when(far == 1)(lambda: own_sent(h))
        pl.when(far > 1)(lambda: sent(far - 1, h))

        @pl.when(after < chips)
        def _():
            pair_copy(after, h).wait_recv()
            absorb(after, h)

        @pl.when(before >= 0)
        def _():
            pair_copy(before, h).wait_recv()
            absorb(before, h)

        pl.when(far == chips - 1)(lambda: finish(h))
        return 0

    lax.fori_loop(0, kvh, own_tokens, 0)
    lax.fori_loop(0, kvh, own_chip, 0)
    forward(0)
    lax.fori_loop(0, kvh * (chips - 1), step, 0)
    for h in range(kvh):
        sent(chips - 1, h)
        out_copy(h).wait()


def body(chips, queries, new_keys, new_values, prefix_keys, prefix_values, block_table, prefix_blocks):
    tokens, width = queries.shape
    kvh = new_keys.shape[1] // DH
    group = width // DH // kvh
    rows = group * tokens
    entries = block_table.shape[1]
    smem = pl.BlockSpec(memory_space=pltpu.SMEM)
    anywhere = pl.BlockSpec(memory_space=pl.ANY)
    dma = pltpu.SemaphoreType.DMA
    keys = (2 * chips + 1) * BS
    return pl.pallas_call(
        functools.partial(kernel, chips, kvh, group, entries),
        out_shape=jax.ShapeDtypeStruct((tokens, width), jnp.bfloat16),
        in_specs=[smem, smem] + [anywhere] * 5,
        out_specs=anywhere,
        scratch_shapes=[
            pltpu.VMEM((kvh, rows, DH), jnp.bfloat16),
            pltpu.VMEM((kvh, 2, tokens, DH), jnp.bfloat16),
            pltpu.VMEM((chips, kvh, 2, 2, BS, DH), jnp.bfloat16),
            pltpu.VMEM((kvh, rows, DH), jnp.float32),
            pltpu.VMEM((kvh, rows, DH), jnp.float32),
            pltpu.VMEM((kvh, rows, DH), jnp.float32),
            pltpu.VMEM((kvh, tokens, rows), jnp.bfloat16),
            pltpu.SMEM((2 * chips,), jnp.float32),
            dma((kvh,)),
            dma((kvh,)),
            dma((kvh,)),
            dma((kvh,)),
            dma((chips, kvh)),
            dma((chips, kvh)),
            dma((chips, kvh)),
            dma((kvh,)),
            dma((chips, kvh)),
        ],
        compiler_params=pltpu.CompilerParams(
            collective_id=0, has_side_effects=True, vmem_limit_bytes=48 * 1024 * 1024
        ),
        cost_estimate=pl.CostEstimate(
            flops=4 * kvh * rows * keys * DH, bytes_accessed=4 * tokens * width, transcendentals=kvh * rows * keys
        ),
    )(block_table, prefix_blocks, queries, new_keys, new_values, prefix_keys, prefix_values)


def solution(mesh):
    rows = P(("grp", "blk"), None)
    return jax.shard_map(
        functools.partial(body, mesh.shape["blk"] // 2),
        mesh=mesh,
        in_specs=(rows,) * 6 + (P(("grp", "blk")),),
        out_specs=rows,
        check_vma=False,
    )
```

time: 145 us -> 34.2 us (0.24)
  waiting for transfers between devices: 41.4 us -> 0 us
  matrix products: 39.5 us -> 0 us
  Pallas kernels: 0 us -> 27.5 us
  local copies, waits for them, and re-layouts: 22.7 us -> 5.81 us
  loops' own time: 16 us -> 0 us
  between operations: 14.2 us -> 0.7 us
  other arithmetic: 10.4 us -> 0 us
    all_gather x2 -> x0, waiting for transfers between devices: 40 us -> none  [the longest x1 21.2 us: body(): piece_values = lax.all_gather(prefix_values, 'blk', axis=0, tiled=True)]
    dot_general x18 -> x0, matrix products: 39.5 us -> none  [the longest x8 22.2 us: absorb(): jnp.einsum('krl,kld->krd', weights.astype(jnp.bfloat16), value_block, pre...]
    pallas_call x0 -> x1, Pallas kernels: none -> 27.5 us  [body(): pl.pallas_call(functools.partial(kernel, chips, kvh, group, entries), out...]
    another operation x1 -> x0, loops' own time: 16 us -> none  [body(): state, _ = lax.scan(visit, state, (key_blocks, value_blocks, block_ids))]
    dynamic_slice x16 -> x0, local copies, waits for them, and re-layouts: 9.4 us -> none  [the longest x8 4.71 us: visit(): used[block_id]]
    reduce_sum x9 -> x0, other arithmetic: 9.27 us -> none  [the longest x8 8.78 us: absorb(): total = factor * total + jnp.sum(weights, axis=-1)]
    transpose x2 -> x0, local copies, waits for them, and re-layouts: 4.99 us -> none  [the longest x1 2.52 us: body(): key_blocks = piece_keys.reshape(count, BS, KVH, DH).transpose(0, 2, 1, 3)]
    reshape x3 -> x0, local copies, waits for them, and re-layouts: 4.67 us -> none  [the longest x1 2.13 us: body(): piece_values.reshape(count, BS, KVH, DH).transpose(0, 2, 1, 3)]
  transfers between devices with their start and end apart: 2 -> 0, of which waited for: 2 -> 0; matrix products, arithmetic and copies ran while one was open for 6% -> 0% of each run, Pallas kernels for 0% -> 0%
where the time goes in v1:
time: 34.2 us; the launch traced here: 34 us
  Pallas kernels  27.5 us (80%)
  local copies, waits for them, and re-layouts  5.81 us (17%)
  between operations  0.7 us (2%)
    pallas_call x1, Pallas kernels, body(): pl.pallas_call(functools.partial(kernel, chips, kvh, group, entries), out...  27.5 us
    unnamed x13, local copies, waits for them, and re-layouts  5.81 us

profile of v1, /device:TPU:0, one launch (start us, length us, event | category | flops | bytes accessed | tf_op | source)
XLA Modules:
  0.0 34.0 jit_solution(16116453270124153761)
XLA Ops:
  0.0 0.0 copy-start.5
  0.7 0.0 copy-done.5
  0.7 0.0 copy-start
  0.7 1.2 %copy-done = bf16[128,4096]{1,0:T(8,128)(2,1)S(1)} copy-done((bf16[128,4096]{1,0:T(8,128)(2,1)S(1)}, bf16[128,4096]{1,0:T(8,128)(2,1)}, u32[]{:S(2)}) %copy-start) | copy-done | bytes 1048600
  1.9 0.0 copy-start.1
  1.9 0.9 %copy-done.1 = bf16[128,512]{1,0:T(8,128)(2,1)S(1)} copy-done((bf16[128,512]{1,0:T(8,128)(2,1)S(1)}, bf16[128,512]{1,0:T(8,128)(2,1)}, u32[]{:S(2)}) %copy-start.1) | copy-done | bytes 131096
  2.8 0.0 copy-start.2
  2.8 0.9 %copy-done.2 = bf16[128,512]{1,0:T(8,128)(2,1)S(1)} copy-done((bf16[128,512]{1,0:T(8,128)(2,1)S(1)}, bf16[128,512]{1,0:T(8,128)(2,1)}, u32[]{:S(2)}) %copy-start.2) | copy-done | bytes 131096
  3.7 0.0 copy-start.3
  3.7 0.9 %copy-done.3 = bf16[128,512]{1,0:T(8,128)(2,1)S(1)} copy-done((bf16[128,512]{1,0:T(8,128)(2,1)S(1)}, bf16[128,512]{1,0:T(8,128)(2,1)}, u32[]{:S(2)}) %copy-start.3) | copy-done | bytes 131096
  4.6 0.0 copy-start.4
  4.6 0.9 %copy-done.4 = bf16[128,512]{1,0:T(8,128)(2,1)S(1)} copy-done((bf16[128,512]{1,0:T(8,128)(2,1)S(1)}, bf16[128,512]{1,0:T(8,128)(2,1)}, u32[]{:S(2)}) %copy-start.4) | copy-done | bytes 131096
  5.5 27.5 %shard_map.73 = bf16[128,4096]{1,0:T(8,128)(2,1)S(1)} custom-call(s32[1,8]{1,0:T(1,128)S(1)} %copy-done.5, s32[1]{0:T(128)S(6)} %copy.9.length_ref, bf16[128,4096]{1,0:T(8,128)(2,1)S(1)} %copy-done, bf16[128,512]{1,0:T(8,128)(2,1)S(1)} %copy-done.1, bf16[128,512]{1,0:T(8,128)(2,1)S(1)} %copy-done.2, bf16[128,512]{1,0:T(8,128)(2,1)S(1)} %copy-done.3, ...), custom_call_target="tpu_custom_call" | custom-call | flops 2415919104 | bytes 2097152 | tf_op jit(solution)/shard_map/pallas_call | solution.py:217
  33.0 1.0 %copy.10 = bf16[128,4096]{1,0:T(8,128)(2,1)} copy(bf16[128,4096]{1,0:T(8,128)(2,1)S(1)} %shard_map.73) | data formatting | bytes 2097152
Async XLA Ops:
  0.0 0.7 %copy-start.5 = (s32[1,8]{1,0:T(1,128)S(1)}, s32[1,8]{1,0:T(1,128)}, u32[]{:S(2)}) copy-start(s32[1,8]{1,0:T(1,128)} %table_ref.1) | copy-start | bytes 100
  0.7 1.2 %copy-start = (bf16[128,4096]{1,0:T(8,128)(2,1)S(1)}, bf16[128,4096]{1,0:T(8,128)(2,1)}, u32[]{:S(2)}) copy-start(bf16[128,4096]{1,0:T(8,128)(2,1)} %q_hbm.1) | copy-start | bytes 3145732
  1.9 0.9 %copy-start.1 = (bf16[128,512]{1,0:T(8,128)(2,1)S(1)}, bf16[128,512]{1,0:T(8,128)(2,1)}, u32[]{:S(2)}) copy-start(bf16[128,512]{1,0:T(8,128)(2,1)} %nk_hbm.1) | copy-start | bytes 393220
  2.8 0.9 %copy-start.2 = (bf16[128,512]{1,0:T(8,128)(2,1)S(1)}, bf16[128,512]{1,0:T(8,128)(2,1)}, u32[]{:S(2)}) copy-start(bf16[128,512]{1,0:T(8,128)(2,1)} %nv_hbm.1) | copy-start | bytes 393220
  3.7 0.9 %copy-start.3 = (bf16[128,512]{1,0:T(8,128)(2,1)S(1)}, bf16[128,512]{1,0:T(8,128)(2,1)}, u32[]{:S(2)}) copy-start(bf16[128,512]{1,0:T(8,128)(2,1)} %pk_hbm.1) | copy-start | bytes 393220
  4.6 0.9 %copy-start.4 = (bf16[128,512]{1,0:T(8,128)(2,1)S(1)}, bf16[128,512]{1,0:T(8,128)(2,1)}, u32[]{:S(2)}) copy-start(bf16[128,512]{1,0:T(8,128)(2,1)} %pv_hbm.1) | copy-start | bytes 393220

commit v2 on v1

--- a/solution.py
+++ b/solution.py
@@ -12,13 +12,13 @@
 MESH = pl.DeviceIdType.MESH
 LOG2E = 1.4426950408889634
 HIDDEN = 1e38
-ROWS = 256
+COLS = 256
 
 
 def kernel(
     chips, kvh, group, entries,
     table_ref, length_ref, q_hbm, nk_hbm, nv_hbm, pk_hbm, pv_hbm, out_hbm,
-    qs, own, kv, acc, top, total, out, penalty,
+    qs, qt, own, kv, acc, top, total, out, penalty,
     q_sem, own_sem, load_sem, out_sem, recv_line, recv_pair, send_line, send_right, send_pair,
 ):
     me = lax.axis_index("blk")
@@ -46,10 +46,7 @@
         cols = pl.ds(h * DH, DH)
         pltpu.make_async_copy(nk_hbm.at[:, cols], own.at[h, 0], own_sem.at[h]).start()
         pltpu.make_async_copy(nv_hbm.at[:, cols], own.at[h, 1], own_sem.at[h]).start()
-        for g in range(group):
-            pltpu.make_async_copy(
-                q_hbm.at[:, pl.ds((h * group + g) * DH, DH)], qs.at[h, pl.ds(g * BS, BS)], q_sem.at[h]
-            ).start()
+        pltpu.make_async_copy(q_hbm.at[:, pl.ds(h * rows, rows)], qs.at[h], q_sem.at[h]).start()
 
     def line_copy(source, h, device, sem):
         piece = kv.at[source, h, :, core]
@@ -87,43 +84,50 @@
         hits = [(table_ref[0, j] == b) & (j < length) for j in range(entries)]
         penalty[b] = jnp.where(functools.reduce(jnp.logical_or, hits), 0.0, HIDDEN)
 
-    def scores_of(query, keys):
-        return lax.dot_general(query, keys, (((1,), (1,)), ((), ())), preferred_element_type=jnp.float32)
-
     def own_tokens(h, _):
         pltpu.make_async_copy(qs.at[h], qs.at[h], q_sem.at[h]).wait()
         pltpu.make_async_copy(own.at[h], own.at[h], own_sem.at[h]).wait()
-        keys, values = own[h, 0], own[h, 1]
-        token = lax.broadcasted_iota(jnp.int32, (ROWS, BS), 0) % BS
-        causal = lax.broadcasted_iota(jnp.int32, (ROWS, BS), 1) <= token
-        for r in range(0, rows, ROWS):
-            at = pl.ds(r, ROWS)
-            scores = jnp.where(causal, scores_of(qs[h, at], keys), -HIDDEN)
-            best = jnp.broadcast_to(jnp.max(scores, axis=-1, keepdims=True), (ROWS, DH))
-            weights = jnp.exp2((scores - best) * factor)
-            top[h, at] = best
-            total[h, at] = weights
-            acc[h, at] = jnp.dot(weights.astype(jnp.bfloat16), values, preferred_element_type=jnp.float32)
+        for g in range(group):
+            at = pl.ds(g * BS, BS)
+            qt[h, :, at] = jnp.transpose(qs[h, :, at])
+        keys, values = own[h, 0], jnp.transpose(own[h, 1])
+        token = lax.broadcasted_iota(jnp.int32, (BS, COLS), 1) % BS
+        causal = lax.broadcasted_iota(jnp.int32, (BS, COLS), 0) <= token
+        for c in range(0, rows, COLS):
+            at = pl.ds(c, COLS)
+            scores = jnp.dot(keys, qt[h, :, at], preferred_element_type=jnp.float32)
+            scores = jnp.where(causal, scores, -HIDDEN).reshape(BS // 8, 8, COLS)
+            best = jnp.max(jnp.max(scores, axis=0), axis=0, keepdims=True)
+            best = jnp.broadcast_to(best, (8, COLS))
+            weights = jnp.exp2((scores - best[None]) * factor)
+            top[h, :, at] = best
+            total[h, :, at] = jnp.sum(weights, axis=0)
+            weights = weights.reshape(BS, COLS).astype(jnp.bfloat16)
+            acc[h, :, at] = jnp.dot(values, weights, preferred_element_type=jnp.float32)
         return 0
 
     def absorb(source, h):
         keys = kv[source, h, 0].reshape(2 * BS, DH)
-        values = kv[source, h, 1].reshape(2 * BS, DH)
+        values = jnp.transpose(kv[source, h, 1].reshape(2 * BS, DH))
         low, high = penalty[2 * source], penalty[2 * source + 1]
-        for r in range(0, rows, ROWS):
-            at = pl.ds(r, ROWS)
-            scores = scores_of(qs[h, at], keys)
-            first, second = scores[:, :BS] - low, scores[:, BS:] - high
-            old = top[h, at]
-            best = jnp.max(jnp.maximum(first, second), axis=-1, keepdims=True)
-            best = jnp.maximum(old, jnp.broadcast_to(best, (ROWS, DH)))
+        for c in range(0, rows, COLS):
+            at = pl.ds(c, COLS)
+            scores = jnp.dot(keys, qt[h, :, at], preferred_element_type=jnp.float32)
+            scores = scores.reshape(2, BS // 8, 8, COLS)
+            peak = jnp.max(scores, axis=1)
+            best = jnp.max(jnp.maximum(peak[0] - low, peak[1] - high), axis=0, keepdims=True)
+            old = top[h, :, at]
+            best = jnp.maximum(old, jnp.broadcast_to(best, (8, COLS)))
             shrink = jnp.exp2((old - best) * factor)
-            first = jnp.exp2((first - best) * factor)
-            second = jnp.exp2((second - best) * factor)
-            top[h, at] = best
-            total[h, at] = shrink * total[h, at] + (first + second)
-            weights = jnp.concatenate([first.astype(jnp.bfloat16), second.astype(jnp.bfloat16)], axis=1)
-            acc[h, at] = shrink * acc[h, at] + jnp.dot(weights, values, preferred_element_type=jnp.float32)
+            first = jnp.exp2((scores[0] - (best + low)[None]) * factor)
+            second = jnp.exp2((scores[1] - (best + high)[None]) * factor)
+            top[h, :, at] = best
+            total[h, :, at] = shrink * total[h, :, at] + (jnp.sum(first, axis=0) + jnp.sum(second, axis=0))
+            weights = jnp.concatenate(
+                [first.reshape(BS, COLS).astype(jnp.bfloat16), second.reshape(BS, COLS).astype(jnp.bfloat16)], axis=0
+            )
+            kept = (acc[h, :, at].reshape(DH // 8, 8, COLS) * shrink[None]).reshape(DH, COLS)
+            acc[h, :, at] = kept + jnp.dot(values, weights, preferred_element_type=jnp.float32)
 
     def out_copy(h):
         cols = pl.ds(pl.multiple_of(h * rows, DH), rows)
@@ -132,8 +136,8 @@
     def finish(h):
         for g in range(group):
             at = pl.ds(g * BS, BS)
-            whole = jnp.sum(total[h, at], axis=-1, keepdims=True)
-            out[h, :, g * DH:(g + 1) * DH] = (acc[h, at] / whole).astype(jnp.bfloat16)
+            share = 1.0 / jnp.sum(total[h, :, at], axis=0, keepdims=True)
+            out[h, :, at] = jnp.transpose(acc[h, :, at] * share).astype(jnp.bfloat16)
         out_copy(h).start()
 
     def own_chip(h, _):
@@ -211,21 +215,22 @@
     rows = group * tokens
     entries = block_table.shape[1]
     smem = pl.BlockSpec(memory_space=pltpu.SMEM)
-    anywhere = pl.BlockSpec(memory_space=pl.ANY)
+    hbm = pl.BlockSpec(memory_space=pltpu.HBM)
     dma = pltpu.SemaphoreType.DMA
     keys = (2 * chips + 1) * BS
     return pl.pallas_call(
         functools.partial(kernel, chips, kvh, group, entries),
         out_shape=jax.ShapeDtypeStruct((tokens, width), jnp.bfloat16),
-        in_specs=[smem, smem] + [anywhere] * 5,
-        out_specs=anywhere,
+        in_specs=[smem, smem] + [hbm] * 5,
+        out_specs=hbm,
         scratch_shapes=[
-            pltpu.VMEM((kvh, rows, DH), jnp.bfloat16),
+            pltpu.VMEM((kvh, tokens, rows), jnp.bfloat16),
+            pltpu.VMEM((kvh, DH, rows), jnp.bfloat16),
             pltpu.VMEM((kvh, 2, tokens, DH), jnp.bfloat16),
             pltpu.VMEM((chips, kvh, 2, 2, BS, DH), jnp.bfloat16),
-            pltpu.VMEM((kvh, rows, DH), jnp.float32),
-            pltpu.VMEM((kvh, rows, DH), jnp.float32),
-            pltpu.VMEM((kvh, rows, DH), jnp.float32),
+            pltpu.VMEM((kvh, DH, rows), jnp.float32),
+            pltpu.VMEM((kvh, 8, rows), jnp.float32),
+            pltpu.VMEM((kvh, 8, rows), jnp.float32),
             pltpu.VMEM((kvh, tokens, rows), jnp.bfloat16),
             pltpu.SMEM((2 * chips,), jnp.float32),
             dma((kvh,)),
@@ -239,7 +244,7 @@
             dma((chips, kvh)),
         ],
         compiler_params=pltpu.CompilerParams(
-            collective_id=0, has_side_effects=True, vmem_limit_bytes=48 * 1024 * 1024
+            collective_id=0, has_side_effects=True, vmem_limit_bytes=60 * 1024 * 1024
         ),
         cost_estimate=pl.CostEstimate(
             flops=4 * kvh * rows * keys * DH, bytes_accessed=4 * tokens * width, transcendentals=kvh * rows * keys

time: 34.2 us -> 37.4 us (1.094)
  Pallas kernels: 27.5 us -> 34.2 us
  local copies, waits for them, and re-layouts: 5.81 us -> 2.29 us
    pallas_call x1, Pallas kernels: 27.5 us -> 34.2 us  [body(): pl.pallas_call(functools.partial(kernel, chips, kvh, group, entries), out...]
    unnamed x13 -> x1, local copies, waits for them, and re-layouts: 5.81 us -> 2.29 us
where the time goes in v2:
time: 37.4 us; the launch traced here: 37.2 us
  Pallas kernels  34.2 us (91%)
  local copies, waits for them, and re-layouts  2.29 us (6%)
  between operations  0.66 us (2%)
    pallas_call x1, Pallas kernels, body(): pl.pallas_call(functools.partial(kernel, chips, kvh, group, entries), out...  34.2 us
    unnamed x1, local copies, waits for them, and re-layouts  2.29 us

profile of v2, /device:TPU:0, one launch (start us, length us, event | category | flops | bytes accessed | tf_op | source)
XLA Modules:
  0.0 37.2 jit_solution(7302297116907193098)
XLA Ops:
  0.7 34.2 %shard_map.73 = bf16[128,4096]{1,0:T(8,128)(2,1)} custom-call(s32[1,8]{1,0:T(1,128)} %table_ref.1, s32[1]{0:T(128)S(6)} %copy.9.length_ref, bf16[128,4096]{1,0:T(8,128)(2,1)} %q_hbm.1, bf16[128,512]{1,0:T(8,128)(2,1)} %nk_hbm.1, bf16[128,512]{1,0:T(8,128)(2,1)} %nv_hbm.1, bf16[128,512]{1,0:T(8,128)(2,1)} %pk_hbm.1, bf16[128,512]{1,0:T(8,128)(2,1)} %pv_hbm.1), custom_call_target="tpu_custom_call" | custom-call | flops 2415919104 | bytes 2097152 | tf_op jit(solution)/shard_map/pallas_call | solution.py:221
  34.9 2.3 %copy.10 = bf16[128,4096]{1,0:T(8,128)(2,1)} copy(bf16[128,4096]{1,0:T(8,128)(2,1)} %shard_map.73) | data formatting | bytes 2097152

commit v3 on v1

--- a/solution.py
+++ b/solution.py
@@ -12,7 +12,6 @@
 MESH = pl.DeviceIdType.MESH
 LOG2E = 1.4426950408889634
 HIDDEN = 1e38
-ROWS = 256
 
 
 def kernel(
@@ -93,37 +92,34 @@
     def own_tokens(h, _):
         pltpu.make_async_copy(qs.at[h], qs.at[h], q_sem.at[h]).wait()
         pltpu.make_async_copy(own.at[h], own.at[h], own_sem.at[h]).wait()
-        keys, values = own[h, 0], own[h, 1]
-        token = lax.broadcasted_iota(jnp.int32, (ROWS, BS), 0) % BS
-        causal = lax.broadcasted_iota(jnp.int32, (ROWS, BS), 1) <= token
-        for r in range(0, rows, ROWS):
-            at = pl.ds(r, ROWS)
-            scores = jnp.where(causal, scores_of(qs[h, at], keys), -HIDDEN)
-            best = jnp.broadcast_to(jnp.max(scores, axis=-1, keepdims=True), (ROWS, DH))
-            weights = jnp.exp2((scores - best) * factor)
-            top[h, at] = best
-            total[h, at] = weights
-            acc[h, at] = jnp.dot(weights.astype(jnp.bfloat16), values, preferred_element_type=jnp.float32)
+        token = lax.broadcasted_iota(jnp.int32, (rows, BS), 0) % BS
+        causal = lax.broadcasted_iota(jnp.int32, (rows, BS), 1) <= token
+        scores = jnp.where(causal, scores_of(qs[h], own[h, 0]), -HIDDEN)
+        best = jnp.broadcast_to(jnp.max(scores, axis=-1, keepdims=True), (rows, DH))
+        weights = jnp.exp2((scores - best) * factor)
+        summed = jnp.dot(weights.astype(jnp.bfloat16), own[h, 1], preferred_element_type=jnp.float32)
+        top[h] = best
+        total[h] = weights
+        acc[h] = summed
         return 0
 
     def absorb(source, h):
         keys = kv[source, h, 0].reshape(2 * BS, DH)
         values = kv[source, h, 1].reshape(2 * BS, DH)
         low, high = penalty[2 * source], penalty[2 * source + 1]
-        for r in range(0, rows, ROWS):
-            at = pl.ds(r, ROWS)
-            scores = scores_of(qs[h, at], keys)
-            first, second = scores[:, :BS] - low, scores[:, BS:] - high
-            old = top[h, at]
-            best = jnp.max(jnp.maximum(first, second), axis=-1, keepdims=True)
-            best = jnp.maximum(old, jnp.broadcast_to(best, (ROWS, DH)))
-            shrink = jnp.exp2((old - best) * factor)
-            first = jnp.exp2((first - best) * factor)
-            second = jnp.exp2((second - best) * factor)
-            top[h, at] = best
-            total[h, at] = shrink * total[h, at] + (first + second)
-            weights = jnp.concatenate([first.astype(jnp.bfloat16), second.astype(jnp.bfloat16)], axis=1)
-            acc[h, at] = shrink * acc[h, at] + jnp.dot(weights, values, preferred_element_type=jnp.float32)
+        old, old_total, old_acc = top[h], total[h], acc[h]
+        scores = scores_of(qs[h], keys)
+        first, second = scores[:, :BS] - low, scores[:, BS:] - high
+        best = jnp.max(jnp.maximum(first, second), axis=-1, keepdims=True)
+        best = jnp.maximum(old, jnp.broadcast_to(best, (rows, DH)))
+        shrink = jnp.exp2((old - best) * factor)
+        first = jnp.exp2((first - best) * factor)
+        second = jnp.exp2((second - best) * factor)
+        weights = jnp.concatenate([first.astype(jnp.bfloat16), second.astype(jnp.bfloat16)], axis=1)
+        summed = jnp.dot(weights, values, preferred_element_type=jnp.float32)
+        top[h] = best
+        total[h] = shrink * old_total + (first + second)
+        acc[h] = shrink * old_acc + summed
 
     def out_copy(h):
         cols = pl.ds(pl.multiple_of(h * rows, DH), rows)
@@ -239,7 +235,7 @@
             dma((chips, kvh)),
         ],
         compiler_params=pltpu.CompilerParams(
-            collective_id=0, has_side_effects=True, vmem_limit_bytes=48 * 1024 * 1024
+            collective_id=0, has_side_effects=True, vmem_limit_bytes=60 * 1024 * 1024
         ),
         cost_estimate=pl.CostEstimate(
             flops=4 * kvh * rows * keys * DH, bytes_accessed=4 * tokens * width, transcendentals=kvh * rows * keys

time: 34.2 us -> 29.1 us (0.85)
  local copies, waits for them, and re-layouts: 5.81 us -> 2.29 us
  Pallas kernels: 27.5 us -> 25.9 us
    unnamed x13 -> x1, local copies, waits for them, and re-layouts: 5.81 us -> 2.29 us
    pallas_call x1, Pallas kernels: 27.5 us -> 25.9 us  [body(): pl.pallas_call(functools.partial(kernel, chips, kvh, group, entries), out...]
where the time goes in v3:
time: 29.1 us; the launch traced here: 28.8 us
  Pallas kernels  25.9 us (89%)
  local copies, waits for them, and re-layouts  2.29 us (8%)
  between operations  0.66 us (2%)
    pallas_call x1, Pallas kernels, body(): pl.pallas_call(functools.partial(kernel, chips, kvh, group, entries), out...  25.9 us
    unnamed x1, local copies, waits for them, and re-layouts  2.29 us

profile of v3, /device:TPU:0, one launch (start us, length us, event | category | flops | bytes accessed | tf_op | source)
XLA Modules:
  0.0 28.8 jit_solution(13379497138578420939)
XLA Ops:
  0.7 25.9 %shard_map.73 = bf16[128,4096]{1,0:T(8,128)(2,1)} custom-call(s32[1,8]{1,0:T(1,128)} %table_ref.1, s32[1]{0:T(128)S(6)} %copy.9.length_ref, bf16[128,4096]{1,0:T(8,128)(2,1)} %q_hbm.1, bf16[128,512]{1,0:T(8,128)(2,1)} %nk_hbm.1, bf16[128,512]{1,0:T(8,128)(2,1)} %nv_hbm.1, bf16[128,512]{1,0:T(8,128)(2,1)} %pk_hbm.1, bf16[128,512]{1,0:T(8,128)(2,1)} %pv_hbm.1), custom_call_target="tpu_custom_call" | custom-call | flops 2415919104 | bytes 2097152 | tf_op jit(solution)/shard_map/pallas_call | solution.py:213
  26.5 2.3 %copy.10 = bf16[128,4096]{1,0:T(8,128)(2,1)} copy(bf16[128,4096]{1,0:T(8,128)(2,1)} %shard_map.73) | data formatting | bytes 2097152

commit v4 on v3

--- a/solution.py
+++ b/solution.py
@@ -16,9 +16,9 @@
 
 def kernel(
     chips, kvh, group, entries,
-    table_ref, length_ref, q_hbm, nk_hbm, nv_hbm, pk_hbm, pv_hbm, out_hbm,
-    qs, own, kv, acc, top, total, out, penalty,
-    q_sem, own_sem, load_sem, out_sem, recv_line, recv_pair, send_line, send_right, send_pair,
+    table_ref, length_ref, q_hbm, nk_hbm, nv_hbm, pk_hbm, pv_hbm, out,
+    qs, own, kv, acc, top, total, penalty,
+    q_sem, own_sem, load_sem, recv_line, recv_pair, send_line, send_right, send_pair,
 ):
     me = lax.axis_index("blk")
     chip = me // 2
@@ -41,6 +41,37 @@
         cols = pl.ds(h * DH, DH)
         pltpu.make_async_copy(pk_hbm.at[:, cols], kv.at[chip, h, 0, core], load_sem.at[h]).start()
         pltpu.make_async_copy(pv_hbm.at[:, cols], kv.at[chip, h, 1, core], load_sem.at[h]).start()
+    def line_copy(source, h, device, sem):
+        piece = kv.at[source, h, :, core]
+        return pltpu.make_async_remote_copy(
+            src_ref=piece, dst_ref=piece, send_sem=sem, recv_sem=recv_line.at[source, h],
+            device_id={"blk": device}, device_id_type=MESH,
+        )
+
+    def pair_copy(source, h):
+        piece = kv.at[source, h, :, core]
+        return pltpu.make_async_remote_copy(
+            src_ref=piece, dst_ref=piece, send_sem=send_pair.at[source, h], recv_sem=recv_pair.at[source, h],
+            device_id={"blk": partner}, device_id_type=MESH,
+        )
+
+    def to_left(source, h):
+        return line_copy(source, h, me - 2, send_line.at[source, h])
+
+    def to_right(source, h):
+        return line_copy(source, h, me + 2, send_line.at[source, h])
+
+    def own_right(h):
+        return line_copy(chip, h, me + 2, send_right.at[h])
+
+    pl.semaphore_wait(barrier, 1 + has_left.astype(jnp.int32) + has_right.astype(jnp.int32))
+    for h in range(kvh):
+        piece = kv.at[chip, h, :, core]
+        pltpu.make_async_copy(piece, piece, load_sem.at[h]).wait()
+        pl.when(has_left)(lambda: to_left(chip, h).start())
+        pl.when(has_right)(lambda: own_right(h).start())
+        pair_copy(chip, h).start()
+
     for h in range(kvh):
         cols = pl.ds(h * DH, DH)
         pltpu.make_async_copy(nk_hbm.at[:, cols], own.at[h, 0], own_sem.at[h]).start()
@@ -49,37 +80,6 @@
             pltpu.make_async_copy(
                 q_hbm.at[:, pl.ds((h * group + g) * DH, DH)], qs.at[h, pl.ds(g * BS, BS)], q_sem.at[h]
             ).start()
-
-    def line_copy(source, h, device, sem):
-        piece = kv.at[source, h, :, core]
-        return pltpu.make_async_remote_copy(
-            src_ref=piece, dst_ref=piece, send_sem=sem, recv_sem=recv_line.at[source, h],
-            device_id={"blk": device}, device_id_type=MESH,
-        )
-
-    def pair_copy(source, h):
-        piece = kv.at[source, h, :, core]
-        return pltpu.make_async_remote_copy(
-            src_ref=piece, dst_ref=piece, send_sem=send_pair.at[source, h], recv_sem=recv_pair.at[source, h],
-            device_id={"blk": partner}, device_id_type=MESH,
-        )
-
-    def to_left(source, h):
-        return line_copy(source, h, me - 2, send_line.at[source, h])
-
-    def to_right(source, h):
-        return line_copy(source, h, me + 2, send_line.at[source, h])
-
-    def own_right(h):
-        return line_copy(chip, h, me + 2, send_right.at[h])
-
-    pl.semaphore_wait(barrier, 1 + has_left.astype(jnp.int32) + has_right.astype(jnp.int32))
-    for h in range(kvh):
-        piece = kv.at[chip, h, :, core]
-        pltpu.make_async_copy(piece, piece, load_sem.at[h]).wait()
-        pl.when(has_left)(lambda: to_left(chip, h).start())
-        pl.when(has_right)(lambda: own_right(h).start())
-        pair_copy(chip, h).start()
 
     length = length_ref[0]
     for b in range(2 * chips):
@@ -121,16 +121,12 @@
         total[h] = shrink * old_total + (first + second)
         acc[h] = shrink * old_acc + summed
 
-    def out_copy(h):
-        cols = pl.ds(pl.multiple_of(h * rows, DH), rows)
-        return pltpu.make_async_copy(out.at[h], out_hbm.at[:, cols], out_sem.at[h])
-
     def finish(h):
+        whole = jnp.sum(total[h], axis=-1, keepdims=True)
+        result = (acc[h] * (1.0 / whole)).astype(jnp.bfloat16)
         for g in range(group):
-            at = pl.ds(g * BS, BS)
-            whole = jnp.sum(total[h, at], axis=-1, keepdims=True)
-            out[h, :, g * DH:(g + 1) * DH] = (acc[h, at] / whole).astype(jnp.bfloat16)
-        out_copy(h).start()
+            cols = pl.ds(pl.multiple_of((h * group + g) * DH, DH), DH)
+            out[:, cols] = result[g * BS:(g + 1) * BS]
 
     def own_chip(h, _):
         pair_copy(chip, h).wait_recv()
@@ -197,7 +193,6 @@
     lax.fori_loop(0, kvh * (chips - 1), step, 0)
     for h in range(kvh):
         sent(chips - 1, h)
-        out_copy(h).wait()
 
 
 def body(chips, queries, new_keys, new_values, prefix_keys, prefix_values, block_table, prefix_blocks):
@@ -212,9 +207,9 @@
     keys = (2 * chips + 1) * BS
     return pl.pallas_call(
         functools.partial(kernel, chips, kvh, group, entries),
-        out_shape=jax.ShapeDtypeStruct((tokens, width), jnp.bfloat16),
+        out_shape=pltpu.VMEM((tokens, width), jnp.bfloat16),
         in_specs=[smem, smem] + [anywhere] * 5,
-        out_specs=anywhere,
+        out_specs=pl.BlockSpec(memory_space=pltpu.VMEM),
         scratch_shapes=[
             pltpu.VMEM((kvh, rows, DH), jnp.bfloat16),
             pltpu.VMEM((kvh, 2, tokens, DH), jnp.bfloat16),
@@ -222,9 +217,7 @@
             pltpu.VMEM((kvh, rows, DH), jnp.float32),
             pltpu.VMEM((kvh, rows, DH), jnp.float32),
             pltpu.VMEM((kvh, rows, DH), jnp.float32),
-            pltpu.VMEM((kvh, tokens, rows), jnp.bfloat16),
             pltpu.SMEM((2 * chips,), jnp.float32),
-            dma((kvh,)),
             dma((kvh,)),
             dma((kvh,)),
             dma((kvh,)),
@@ -235,7 +228,7 @@
             dma((chips, kvh)),
         ],
         compiler_params=pltpu.CompilerParams(
-            collective_id=0, has_side_effects=True, vmem_limit_bytes=60 * 1024 * 1024
+            collective_id=0, has_side_effects=True, vmem_limit_bytes=57 * 1024 * 1024
         ),
         cost_estimate=pl.CostEstimate(
             flops=4 * kvh * rows * keys * DH, bytes_accessed=4 * tokens * width, transcendentals=kvh * rows * keys

time: 29.1 us -> 27.5 us (0.945)
  local copies, waits for them, and re-layouts: 2.29 us -> 0.97 us
  Pallas kernels: 25.9 us -> 25.6 us
    unnamed x1, local copies, waits for them, and re-layouts: 2.29 us -> 0.97 us
    pallas_call x1, Pallas kernels: 25.9 us -> 25.6 us  [body(): pl.pallas_call(functools.partial(kernel, chips, kvh, group, entries), out...]
where the time goes in v4:
time: 27.5 us; the launch traced here: 27.2 us
  Pallas kernels  25.6 us (93%)
  local copies, waits for them, and re-layouts  0.97 us (4%)
  between operations  0.66 us (2%)
    pallas_call x1, Pallas kernels, body(): pl.pallas_call(functools.partial(kernel, chips, kvh, group, entries), out...  25.6 us
    unnamed x1, local copies, waits for them, and re-layouts  0.97 us

profile of v4, /device:TPU:0, one launch (start us, length us, event | category | flops | bytes accessed | tf_op | source)
XLA Modules:
  0.0 27.2 jit_solution(10414343503068307548)
XLA Ops:
  0.7 25.6 %shard_map.73 = bf16[128,4096]{1,0:T(8,128)(2,1)S(1)} custom-call(s32[1,8]{1,0:T(1,128)} %table_ref.1, s32[1]{0:T(128)S(6)} %copy.10.length_ref, bf16[128,4096]{1,0:T(8,128)(2,1)} %q_hbm.1, bf16[128,512]{1,0:T(8,128)(2,1)} %nk_hbm.1, bf16[128,512]{1,0:T(8,128)(2,1)} %nv_hbm.1, bf16[128,512]{1,0:T(8,128)(2,1)} %pk_hbm.1, bf16[128,512]{1,0:T(8,128)(2,1)} %pv_hbm.1), custom_call_target="tpu_custom_call" | custom-call | flops 2415919104 | bytes 2097152 | tf_op jit(solution)/shard_map/pallas_call | solution.py:208
  26.2 1.0 %copy.9 = bf16[128,4096]{1,0:T(8,128)(2,1)} copy(bf16[128,4096]{1,0:T(8,128)(2,1)S(1)} %shard_map.73) | data formatting | bytes 2097152

commit v5 on v4

--- a/solution.py
+++ b/solution.py
@@ -27,6 +27,8 @@
     rows = group * BS
     factor = LOG2E * DH ** -0.5
     has_left, has_right = chip > 0, chip < chips - 1
+    inner = has_left & has_right
+    items = kvh * (chips - 1)
 
     barrier = pltpu.get_barrier_semaphore()
 
@@ -131,6 +133,7 @@
     def own_chip(h, _):
         pair_copy(chip, h).wait_recv()
         absorb(chip, h)
+        pl.when(inner)(lambda: forward(h))
         return 0
 
     def forward(i):
@@ -170,7 +173,7 @@
     def step(i, _):
         far, h = 1 + i // kvh, i % kvh
         before, after = chip - far, chip + far
-        pl.when(i + 1 < kvh * (chips - 1))(lambda: forward(i + 1))
+        pl.when(jnp.logical_not(inner) & (i + 1 < items))(lambda: forward(i + 1))
         pl.when(far == 1)(lambda: own_sent(h))
         pl.when(far > 1)(lambda: sent(far - 1, h))
 
@@ -184,13 +187,14 @@
             pair_copy(before, h).wait_recv()
             absorb(before, h)
 
+        pl.when(inner & (i + kvh < items))(lambda: forward(i + kvh))
         pl.when(far == chips - 1)(lambda: finish(h))
         return 0
 
     lax.fori_loop(0, kvh, own_tokens, 0)
     lax.fori_loop(0, kvh, own_chip, 0)
-    forward(0)
-    lax.fori_loop(0, kvh * (chips - 1), step, 0)
+    pl.when(jnp.logical_not(inner))(lambda: forward(0))
+    lax.fori_loop(0, items, step, 0)
     for h in range(kvh):
         sent(chips - 1, h)
 

time: 27.5 us -> 27.3 us (level)
  no operation moved by 1% of the time
where the time goes in v5:
time: 27.3 us; the launch traced here: 27.1 us
  Pallas kernels  25.5 us (93%)
  local copies, waits for them, and re-layouts  0.97 us (4%)
  between operations  0.66 us (2%)
    pallas_call x1, Pallas kernels, body(): pl.pallas_call(functools.partial(kernel, chips, kvh, group, entries), out...  25.5 us
    unnamed x1, local copies, waits for them, and re-layouts  0.97 us

profile of v5, /device:TPU:0, one launch (start us, length us, event | category | flops | bytes accessed | tf_op | source)
XLA Modules:
  0.0 27.1 jit_solution(1328487193191745655)
XLA Ops:
  0.7 25.5 %shard_map.73 = bf16[128,4096]{1,0:T(8,128)(2,1)S(1)} custom-call(s32[1,8]{1,0:T(1,128)} %table_ref.1, s32[1]{0:T(128)S(6)} %copy.10.length_ref, bf16[128,4096]{1,0:T(8,128)(2,1)} %q_hbm.1, bf16[128,512]{1,0:T(8,128)(2,1)} %nk_hbm.1, bf16[128,512]{1,0:T(8,128)(2,1)} %nv_hbm.1, bf16[128,512]{1,0:T(8,128)(2,1)} %pk_hbm.1, bf16[128,512]{1,0:T(8,128)(2,1)} %pv_hbm.1), custom_call_target="tpu_custom_call" | custom-call | flops 2415919104 | bytes 2097152 | tf_op jit(solution)/shard_map/pallas_call | solution.py:212
  26.1 1.0 %copy.9 = bf16[128,4096]{1,0:T(8,128)(2,1)} copy(bf16[128,4096]{1,0:T(8,128)(2,1)S(1)} %shard_map.73) | data formatting | bytes 2097152

commit v6 on v5

--- a/solution.py
+++ b/solution.py
@@ -123,6 +123,17 @@
         total[h] = shrink * old_total + (first + second)
         acc[h] = shrink * old_acc + summed
 
+    def absorb_one(source, h, side):
+        old, old_total, old_acc = top[h], total[h], acc[h]
+        scores = scores_of(qs[h], kv[source, h, 0, side]) - penalty[2 * source + side]
+        best = jnp.maximum(old, jnp.broadcast_to(jnp.max(scores, axis=-1, keepdims=True), (rows, DH)))
+        shrink = jnp.exp2((old - best) * factor)
+        weights = jnp.exp2((scores - best) * factor)
+        summed = jnp.dot(weights.astype(jnp.bfloat16), kv[source, h, 1, side], preferred_element_type=jnp.float32)
+        top[h] = best
+        total[h] = shrink * old_total + weights
+        acc[h] = shrink * old_acc + summed
+
     def finish(h):
         whole = jnp.sum(total[h], axis=-1, keepdims=True)
         result = (acc[h] * (1.0 / whole)).astype(jnp.bfloat16)
@@ -173,6 +184,8 @@
     def step(i, _):
         far, h = 1 + i // kvh, i % kvh
         before, after = chip - far, chip + far
+        pl.when(jnp.logical_not(inner) & has_right)(lambda: absorb_one(after, h, core))
+        pl.when(jnp.logical_not(inner) & has_left)(lambda: absorb_one(before, h, core))
         pl.when(jnp.logical_not(inner) & (i + 1 < items))(lambda: forward(i + 1))
         pl.when(far == 1)(lambda: own_sent(h))
         pl.when(far > 1)(lambda: sent(far - 1, h))
@@ -180,12 +193,14 @@
         @pl.when(after < chips)
         def _():
             pair_copy(after, h).wait_recv()
-            absorb(after, h)
+            pl.when(inner)(lambda: absorb(after, h))
+            pl.when(jnp.logical_not(inner))(lambda: absorb_one(after, h, 1 - core))
 
         @pl.when(before >= 0)
         def _():
             pair_copy(before, h).wait_recv()
-            absorb(before, h)
+            pl.when(inner)(lambda: absorb(before, h))
+            pl.when(jnp.logical_not(inner))(lambda: absorb_one(before, h, 1 - core))
 
         pl.when(inner & (i + kvh < items))(lambda: forward(i + kvh))
         pl.when(far == chips - 1)(lambda: finish(h))

time: 27.3 us -> 28.4 us (1.040)
  Pallas kernels: 25.5 us -> 26.5 us
    pallas_call x1, Pallas kernels: 25.5 us -> 26.5 us  [body(): pl.pallas_call(functools.partial(kernel, chips, kvh, group, entries), out...]
where the time goes in v6:
time: 28.4 us; the launch traced here: 28.2 us
  Pallas kernels  26.5 us (93%)
  local copies, waits for them, and re-layouts  0.97 us (3%)
  between operations  0.66 us (2%)
    pallas_call x1, Pallas kernels, body(): pl.pallas_call(functools.partial(kernel, chips, kvh, group, entries), out...  26.5 us
    unnamed x1, local copies, waits for them, and re-layouts  0.97 us

profile of v6, /device:TPU:0, one launch (start us, length us, event | category | flops | bytes accessed | tf_op | source)
XLA Modules:
  0.0 28.2 jit_solution(4627301415190153285)
XLA Ops:
  0.7 26.5 %shard_map.73 = bf16[128,4096]{1,0:T(8,128)(2,1)S(1)} custom-call(s32[1,8]{1,0:T(1,128)} %table_ref.1, s32[1]{0:T(128)S(6)} %copy.10.length_ref, bf16[128,4096]{1,0:T(8,128)(2,1)} %q_hbm.1, bf16[128,512]{1,0:T(8,128)(2,1)} %nk_hbm.1, bf16[128,512]{1,0:T(8,128)(2,1)} %nv_hbm.1, bf16[128,512]{1,0:T(8,128)(2,1)} %pk_hbm.1, bf16[128,512]{1,0:T(8,128)(2,1)} %pv_hbm.1), custom_call_target="tpu_custom_call" | custom-call | flops 2415919104 | bytes 2097152 | tf_op jit(solution)/shard_map/pallas_call | solution.py:227
  27.2 1.0 %copy.9 = bf16[128,4096]{1,0:T(8,128)(2,1)} copy(bf16[128,4096]{1,0:T(8,128)(2,1)S(1)} %shard_map.73) | data formatting | bytes 2097152

commit v7 on v5

--- a/solution.py
+++ b/solution.py
@@ -72,6 +72,7 @@
         pltpu.make_async_copy(piece, piece, load_sem.at[h]).wait()
         pl.when(has_left)(lambda: to_left(chip, h).start())
         pl.when(has_right)(lambda: own_right(h).start())
+    for h in range(kvh):
         pair_copy(chip, h).start()
 
     for h in range(kvh):

time: 27.3 us -> 27.3 us (level)
  no operation moved by 1% of the time
where the time goes in v7:
time: 27.3 us; the launch traced here: 27.1 us
  Pallas kernels  25.4 us (93%)
  local copies, waits for them, and re-layouts  0.97 us (4%)
  between operations  0.66 us (2%)
    pallas_call x1, Pallas kernels, body(): pl.pallas_call(functools.partial(kernel, chips, kvh, group, entries), out...  25.4 us
    unnamed x1, local copies, waits for them, and re-layouts  0.97 us

profile of v7, /device:TPU:0, one launch (start us, length us, event | category | flops | bytes accessed | tf_op | source)
XLA Modules:
  0.0 27.1 jit_solution(18239526953289664749)
XLA Ops:
  0.7 25.4 %shard_map.73 = bf16[128,4096]{1,0:T(8,128)(2,1)S(1)} custom-call(s32[1,8]{1,0:T(1,128)} %table_ref.1, s32[1]{0:T(128)S(6)} %copy.10.length_ref, bf16[128,4096]{1,0:T(8,128)(2,1)} %q_hbm.1, bf16[128,512]{1,0:T(8,128)(2,1)} %nk_hbm.1, bf16[128,512]{1,0:T(8,128)(2,1)} %nv_hbm.1, bf16[128,512]{1,0:T(8,128)(2,1)} %pk_hbm.1, bf16[128,512]{1,0:T(8,128)(2,1)} %pv_hbm.1), custom_call_target="tpu_custom_call" | custom-call | flops 2415919104 | bytes 2097152 | tf_op jit(solution)/shard_map/pallas_call | solution.py:213
  26.1 1.0 %copy.9 = bf16[128,4096]{1,0:T(8,128)(2,1)} copy(bf16[128,4096]{1,0:T(8,128)(2,1)S(1)} %shard_map.73) | data formatting | bytes 2097152
